TPU v7x, 256 devices: a whole 4x4x8 slice. The times are simulated.
256 devices in a mesh: blk: 64 (over x, z, y_hi), col: 4 (over y_lo, core).
Axes of the slice: x: 4, y: 4 (y_hi: 2, y_lo: 2; y = y_hi * 2 + y_lo), z: 8, core: 2. Of those that a mesh axis runs over, the one named last changes fastest.
Arguments:
- node_features: bfloat16 [131072, 128], P(('blk', 'col')), may hold values from -6 to 6
- degree: int32 [131072], P(('blk', 'col')), may hold values from 1 to 8
- adjacency: bfloat16 [92160, 128, 128], P(('blk', 'col')), may hold values from -0.125 to 0.125
- tile_rows: int32 [92160], P(('blk', 'col')), may hold values from 0 to 15
- tile_cols: int32 [92160], P(('blk', 'col')), may hold values from 0 to 3
- counts: int32 [1280], P(('blk', 'col')), may hold values from 1 to 72, as said below
- weight: bfloat16 [128, 256], replicated, may hold values from -0.5 to 0.5
- bias_vector: float32 [256], replicated, may hold values from -3 to 3
- cotangent: bfloat16 [131072, 256], P(('blk', 'col')), may hold values from -6 to 6
Outputs:
- activations: bfloat16 [131072, 256], P(('blk', 'col'))
- grad_features: bfloat16 [131072, 128], P(('blk', 'col'))
- grad_weight: float32 [128, 256], replicated
- grad_bias: float32 [256], replicated
Inputs may be any that keep to these rules, and one draw needn't show every extreme that they name: `counts`: every draw has some pair with all 72 slots live.
All inputs are finite; a program needn't handle non-finite values.
Results may differ from a plain program's by a relative error of at most 0.012.
Values may be sent and summed in bfloat16 or wider, within the bound.
A program may use at most 128 MiB of HBM per device.

v0:
```python
import jax
import jax.numpy as jnp
from jax import lax
from jax.sharding import PartitionSpec as P


def from_behind(value, axis, by):
    length = lax.axis_size(axis)
    return lax.ppermute(value, axis, [(i, (i + by) % length) for i in range(length)])


def shortened(value):

    def short(part):
        return part.astype(jnp.bfloat16) if part.dtype == jnp.float32 else part

    return jax.tree.map(short, value)


def local(
    node_features, degree, adjacency, tile_rows, tile_cols, counts, weight, bias_vector, cotangent
):
    offset_count = counts.shape[0]
    reach_steps = (offset_count - 1) // 2
    tile_size = adjacency.shape[1]
    slot_count = adjacency.shape[0] // offset_count
    own_rows, features = node_features.shape
    own_tiles = own_rows // tile_size
    col_count = lax.axis_size("col")
    block_tiles = col_count * own_tiles
    live_slots = jnp.arange(slot_count)[None, :] < counts[:, None]
    adjacency = adjacency.reshape(offset_count, slot_count, tile_size, tile_size)
    adjacency = jnp.where(live_slots[:, :, None, None], adjacency, jnp.zeros_like(adjacency))
    dest_tiles = tile_rows.reshape(offset_count, slot_count)
    source_tiles = tile_cols.reshape(offset_count, slot_count)
    row_scale = lax.rsqrt(degree.astype(jnp.float32))
    source = (row_scale[:, None] * node_features.astype(jnp.float32)).astype(jnp.bfloat16)
    fetched = [source] * offset_count
    ahead_rows = source
    behind_rows = source
    for distance in range(1, reach_steps + 1):
        ahead_rows = from_behind(ahead_rows, "blk", -1)
        behind_rows = from_behind(behind_rows, "blk", 1)
        fetched[reach_steps + distance] = ahead_rows
        fetched[reach_steps - distance] = behind_rows
    picked = jnp.stack(
        [
            fetched[offset].reshape(own_tiles, tile_size, features)[source_tiles[offset]]
            for offset in range(offset_count)
        ]
    )
    products = jnp.einsum("ksrq,ksqf->ksrf", adjacency, picked, preferred_element_type=jnp.float32)
    block_sums = jax.ops.segment_sum(
        products.reshape(-1, tile_size, features), dest_tiles.reshape(-1), block_tiles
    )
    block_sums = block_sums.reshape(block_tiles * tile_size, features)
    sums = lax.psum_scatter(block_sums, "col", scatter_dimension=0, tiled=True)
    aggregated = (row_scale[:, None] * sums).astype(jnp.bfloat16)
    pre_act = jnp.dot(aggregated, weight, preferred_element_type=jnp.float32) + bias_vector
    gate_value = jax.nn.sigmoid(pre_act)
    activations = (pre_act * gate_value).astype(jnp.bfloat16)
    grad_pre = cotangent.astype(jnp.float32) * gate_value * (1.0 + pre_act * (1.0 - gate_value))
    grad_low = grad_pre.astype(jnp.bfloat16)
    weight_part = lax.dot_general(
        aggregated, grad_low, (((0,), (0,)), ((), ())), preferred_element_type=jnp.float32
    )
    bias_part = jnp.sum(grad_pre, axis=0)
    weight_sum, bias_sum = lax.psum((weight_part, bias_part), ("blk", "col"))
    norm_factor = float(own_rows * lax.axis_size("blk") * col_count) ** (-0.5)
    grad_rows = lax.dot_general(
        grad_low, weight, (((1,), (1,)), ((), ())), preferred_element_type=jnp.float32
    )
    grad_hidden = (row_scale[:, None] * grad_rows).astype(jnp.bfloat16)
    block_grad = lax.all_gather(grad_hidden, "col", axis=0, tiled=True)
    picked_grad = block_grad.reshape(block_tiles, tile_size, features)[dest_tiles]
    back_terms = jnp.einsum(
        "ksrq,ksrf->ksqf", adjacency, picked_grad, preferred_element_type=jnp.float32
    )
    target_ids = jnp.arange(offset_count)[:, None] * own_tiles + source_tiles
    outgoing = jax.ops.segment_sum(
        back_terms.reshape(-1, tile_size, features),
        target_ids.reshape(-1),
        offset_count * own_tiles,
    )
    outgoing = outgoing.reshape(offset_count, own_rows, features)
    total_back = outgoing[reach_steps]
    carry_up = jnp.zeros((own_rows, features), jnp.float32)
    carry_down = jnp.zeros((own_rows, features), jnp.float32)
    for distance in range(reach_steps, 0, -1):
        carry_up = from_behind(shortened(carry_up + outgoing[reach_steps + distance]), "blk", 1)
        carry_down = from_behind(
            shortened(carry_down + outgoing[reach_steps - distance]), "blk", -1
        )
    total_back = total_back + carry_up + carry_down
    grad_features = (row_scale[:, None] * total_back).astype(jnp.bfloat16)
    return (activations, grad_features, weight_sum * norm_factor, bias_sum * norm_factor)


def solution(mesh):
    return jax.shard_map(
        local,
        mesh=mesh,
        in_specs=(
            P(("blk", "col"), None),
            P(("blk", "col")),
            P(("blk", "col"), None, None),
            P(("blk", "col")),
            P(("blk", "col")),
            P(("blk", "col")),
            P(),
            P(),
            P(("blk", "col"), None),
        ),
        out_specs=(P(("blk", "col"), None), P(("blk", "col"), None), P(), P()),
        check_vma=False,
    )
```

profile of v0, /device:TPU:1, one launch (start us, length us, event | category | flops | bytes accessed | tf_op | source)
XLA Modules:
  0.0 485.4 jit_solution(10293052520780361430)
XLA Ops:
  7.9 1.0 multiply_convert_fusion.2
  9.0 3.8 collective-permute-start
  12.8 7.6 %collective-permute-start.2 = (bf16[512,128]{1,0:T(8,128)(2,1)S(1)}, bf16[512,128]{1,0:T(8,128)(2,1)S(1)}, u32[]{:S(2)}, u32[]{:S(2)}) collective-permute-start(bf16[512,128]{1,0:T(8,128)(2,1)S(1)} %multiply_convert_fusion.2), channel_id=1, source_target_pairs={{0,252},{4,0},{8,4},{12,8},{16,12},{20,16},{24,20},{28,24},{32,28}... | collective-permute-start | bytes 393224 | tf_op jit(solution)/shard_map/ppermute | solution.py:9
  22.0 1.5 collective-permute-done
  23.5 16.3 %copy.15 = bf16[5,72,128,128]{2,3,1,0:T(8,128)(2,1)} copy(bf16[5,72,128,128]{3,2,1,0:T(8,128)(2,1)} %bitcast.57) | data formatting | bytes 23592960 | tf_op jit(solution)/shard_map/reshape | solution.py:32
  39.8 1.0 gather_fusion.2
  40.8 2.4 gather_fusion.1
  43.3 2.4 gather_fusion.3
  45.7 7.2 %collective-permute-start.3 = (bf16[512,128]{1,0:T(8,128)(2,1)S(1)}, bf16[512,128]{1,0:T(8,128)(2,1)S(1)}, u32[]{:S(2)}, u32[]{:S(2)}) collective-permute-start(bf16[512,128]{1,0:T(8,128)(2,1)S(1)} %collective-permute-done.2), channel_id=1, source_target_pairs={{0,252},{4,0},{8,4},{12,8},{16,12},{20,16},{24,20},{28,24},{32,28}... | collective-permute-start | bytes 393224 | tf_op jit(solution)/shard_map/ppermute | solution.py:9
  52.9 2.5 gather_fusion
  55.3 2.0 bitcast_dynamic-update-slice_fusion.4
  57.3 2.1 bitcast_dynamic-update-slice_fusion.3
  60.1 4.3 copy-done.3
  64.4 1.0 gather_fusion.4
  65.4 1.6 bitcast_dynamic-update-slice_fusion
  67.0 14.5 %fusion.1 = f32[5,72,128,128]{3,2,1,0:T(8,128)} fusion(bf16[5,72,128,128]{3,2,1,0:T(8,128)(2,1)} %bitcast_dynamic-update-slice_fusion, bf16[5,72,128,128]{2,3,1,0:T(8,128)(2,1)} %copy.15, pred[5,72]{1,0:T(8,128)(4,1)S(1)} %iota_compare_fusion), kind=kOutput, calls=%fused_computation.10 | convolution fusion | flops 1515847680 | bytes 47186280 | tf_op jit(solution)/shard_map/ksrq,ksqf->ksrf/dot_general | solution.py:52
  81.7 47.9 %scatter_fusion = f32[16,128,128]{2,1,0:T(8,128)S(1)} fusion(f32[16,128,128]{2,1,0:T(8,128)S(1)} %broadcast_in_dim.42, s32[360]{0:T(512)S(1)} %copy-done.7, f32[360,128,128]{2,1,0:T(8,128)} %bitcast.50), kind=kCustom, calls=%fused_computation.6 | custom fusion | flops 5898240 | bytes 70780320 | tf_op jit(solution)/shard_map/scatter-add | solution.py:53
  129.7 1.0 copy-done.2
  131.0 18.1 %reduce-scatter.2.cloned.1.call-done = f32[512,128]{1,0:T(8,128)} async-done(((f32[2048,128]{1,0:T(8,128)}), f32[512,128]{1,0:T(8,128)}) %reduce-scatter.2.cloned.1.call-update) | async-done | bytes 262160 | tf_op jit(solution)/shard_map/reduce_scatter | solution.py:57
  149.2 2.1 fusion.15
  151.5 7.5 %all_gather.3 = bf16[2048,128]{1,0:T(8,128)(2,1)S(1)} all-gather(bf16[512,128]{1,0:T(8,128)(2,1)S(1)} %fusion.4), channel_id=1, replica_groups=mesh['blk'=64,'col'=4] {'col'}, dimensions={0}, use_global_device_ids=true | all-gather | bytes 655360 | tf_op jit(solution)/shard_map/all_gather | solution.py:74
  159.0 11.1 %gather_fusion.5 = bf16[360,128,128]{2,1,0:T(8,128)(2,1)} fusion(bf16[16,128,128]{2,1,0:T(8,128)(2,1)S(1)} %bitcast.48, s32[1024]{0:T(1024)S(1)} %pad_clamp_fusion), kind=kCustom, calls=%fused_computation.5 | custom fusion | bytes 23594400 | tf_op jit(solution)/shard_map/gather | solution.py:75
  170.1 15.2 %fusion = f32[5,72,128,128]{3,2,1,0:T(8,128)} fusion(bf16[5,72,128,128]{3,2,1,0:T(8,128)(2,1)} %bitcast.52, bf16[5,72,128,128]{2,3,1,0:T(8,128)(2,1)} %copy.15, pred[5,72]{1,0:T(8,128)(4,1)S(1)} %iota_compare_fusion), kind=kOutput, calls=%fused_computation.9 | convolution fusion | flops 1515847680 | bytes 47186280 | tf_op jit(solution)/shard_map/ksrq,ksrf->ksqf/dot_general | solution.py:76
  185.5 47.9 %scatter_fusion.1 = f32[20,128,128]{2,1,0:T(8,128)S(1)} fusion(f32[20,128,128]{2,1,0:T(8,128)S(1)} %broadcast_in_dim.50, s32[360]{0:T(512)S(1)} %add.88, f32[360,128,128]{2,1,0:T(8,128)} %bitcast.49), kind=kCustom, calls=%fused_computation.7 | custom fusion | flops 5898240 | bytes 70780320 | tf_op jit(solution)/shard_map/scatter-add | solution.py:80
  233.5 1.0 fusion.10
  234.5 2.6 collective-permute-start.4
  237.2 4.8 collective-permute-start.6
  242.0 73.0 %psum.15 = f32[256]{0:T(256)S(1)} all-reduce(f32[256]{0:T(256)S(1)} %get-tuple-element.4), channel_id=1, replica_groups=mesh['blk'=64,'col'=4] {'blk','col'}, use_global_device_ids=true, to_apply=%region_5.6 | all-reduce | flops 256 | bytes 2048 | tf_op jit(solution)/shard_map/psum | solution.py:68
  315.7 1.1 collective-permute-start.5
  316.8 6.2 %collective-permute-start.7 = (bf16[512,128]{1,0:T(8,128)(2,1)S(1)}, bf16[512,128]{1,0:T(8,128)(2,1)S(1)}, u32[]{:S(2)}, u32[]{:S(2)}) collective-permute-start(bf16[512,128]{1,0:T(8,128)(2,1)S(1)} %fusion.5), channel_id=1, source_target_pairs={{0,252},{4,0},{8,4},{12,8},{16,12},{20,16},{24,20},{28,24},{32,28}... | collective-permute-start | bytes 393224 | tf_op jit(solution)/shard_map/ppermute | solution.py:9
  323.0 153.2 %all-reduce.2.cloned.1.call-done = f32[128,256]{1,0:T(8,128)} async-done(((f32[128,256]{1,0:T(8,128)}), f32[128,256]{1,0:T(8,128)}) %all-reduce.2.cloned.1.call-update) | async-done | bytes 131088 | tf_op jit(solution)/shard_map/psum | solution.py:68
  476.2 1.6 broadcast_multiply_fusion
  (57 shorter events, 5.5 us)
Async XLA Ops:
  7.2 142.0 %copy-start = (bf16[128,256]{1,0:T(8,128)(2,1)S(1)}, bf16[128,256]{1,0:T(8,128)(2,1)}, u32[]{:S(2)}) copy-start(bf16[128,256]{1,0:T(8,128)(2,1)} %param.15) | copy-start | bytes 196612
  7.2 142.0 %reduce-scatter.2.cloned.1.call-start = ((), (), s32[]{:S(2)}) async-start(), calls=%async_computation.1 | async-start | bytes 1310720 | tf_op jit(solution)/shard_map/reduce_scatter | solution.py:57
  9.0 14.5 %collective-permute-start = (bf16[512,128]{1,0:T(8,128)(2,1)S(1)}, bf16[512,128]{1,0:T(8,128)(2,1)S(1)}, u32[]{:S(2)}, u32[]{:S(2)}) collective-permute-start(bf16[512,128]{1,0:T(8,128)(2,1)S(1)} %multiply_convert_fusion.2), channel_id=1, source_target_pairs={{0,4},{4,8},{8,12},{12,16},{16,20},{20,24},{24,28},{28,32},{32,36}... | collective-permute-start | bytes 393224 | tf_op jit(solution)/shard_map/ppermute | solution.py:9
  12.8 30.5 %collective-permute-start.2 = (bf16[512,128]{1,0:T(8,128)(2,1)S(1)}, bf16[512,128]{1,0:T(8,128)(2,1)S(1)}, u32[]{:S(2)}, u32[]{:S(2)}) collective-permute-start(bf16[512,128]{1,0:T(8,128)(2,1)S(1)} %multiply_convert_fusion.2), channel_id=1, source_target_pairs={{0,252},{4,0},{8,4},{12,8},{16,12},{20,16},{24,20},{28,24},{32,28}... | collective-permute-start | bytes 393224 | tf_op jit(solution)/shard_map/ppermute | solution.py:9
  23.5 29.4 %collective-permute-start.1 = (bf16[512,128]{1,0:T(8,128)(2,1)S(1)}, bf16[512,128]{1,0:T(8,128)(2,1)S(1)}, u32[]{:S(2)}, u32[]{:S(2)}) collective-permute-start(bf16[512,128]{1,0:T(8,128)(2,1)S(1)} %collective-permute-done), channel_id=1, source_target_pairs={{0,4},{4,8},{8,12},{12,16},{16,20},{20,24},{24,28},{28,32},{32,36}... | collective-permute-start | bytes 393224 | tf_op jit(solution)/shard_map/ppermute | solution.py:9
  45.7 14.4 %collective-permute-start.3 = (bf16[512,128]{1,0:T(8,128)(2,1)S(1)}, bf16[512,128]{1,0:T(8,128)(2,1)S(1)}, u32[]{:S(2)}, u32[]{:S(2)}) collective-permute-start(bf16[512,128]{1,0:T(8,128)(2,1)S(1)} %collective-permute-done.2), channel_id=1, source_target_pairs={{0,252},{4,0},{8,4},{12,8},{16,12},{20,16},{24,20},{28,24},{32,28}... | collective-permute-start | bytes 393224 | tf_op jit(solution)/shard_map/ppermute | solution.py:9
  55.3 4.4 copy-start.4
  60.1 4.3 copy-start.3
  67.0 14.7 %copy-start.7 = (s32[360]{0:T(512)S(1)}, s32[360]{0:T(512)}, u32[]{:S(2)}) copy-start(s32[360]{0:T(512)} %param.12) | copy-start | bytes 4324
  81.7 49.4 %copy-start.6 = (s32[360]{0:T(512)S(1)}, s32[360]{0:T(512)}, u32[]{:S(2)}) copy-start(s32[360]{0:T(512)} %param.13) | copy-start | bytes 4324
  81.7 67.5 %copy-start.8 = (bf16[512,256]{1,0:T(8,128)(2,1)S(1)}, bf16[512,256]{1,0:T(8,128)(2,1)}, u32[]{:S(2)}) copy-start(bf16[512,256]{1,0:T(8,128)(2,1)} %param.17) | copy-start | bytes 786436
  81.7 67.5 %copy-start.9 = (f32[256]{0:T(256)S(1)}, f32[256]{0:T(256)}, u32[]{:S(2)}) copy-start(f32[256]{0:T(256)} %param.16) | copy-start | bytes 3076
  129.7 1.0 copy-start.2
  130.7 345.6 %all-reduce.2.cloned.1.call-start = ((), (), s32[]{:S(2)}) async-start(), calls=%async_computation.2 | async-start | bytes 262144 | tf_op jit(solution)/shard_map/psum | solution.py:68
  185.4 48.1 %copy-start.5 = (f32[512,128]{1,0:T(8,128)S(1)}, f32[512,128]{1,0:T(8,128)}, u32[]{:S(2)}) copy-start(f32[512,128]{1,0:T(8,128)} %reduce-scatter.2.cloned.1.call-done) | copy-start | bytes 786436
  185.5 293.1 %copy-start.1 = (bf16[128,256]{1,0:T(8,128)(2,1)S(1)}, bf16[128,256]{1,0:T(8,128)(2,1)}, u32[]{:S(2)}) copy-start(bf16[128,256]{1,0:T(8,128)(2,1)} %param.15) | copy-start | bytes 196612
  234.5 81.1 %collective-permute-start.4 = (bf16[512,128]{1,0:T(8,128)(2,1)S(1)}, bf16[512,128]{1,0:T(8,128)(2,1)S(1)}, u32[]{:S(2)}, u32[]{:S(2)}) collective-permute-start(bf16[512,128]{1,0:T(8,128)(2,1)S(1)} %bitcast.59), channel_id=1, source_target_pairs={{0,4},{4,8},{8,12},{12,16},{16,20},{20,24},{24,28},{28,32},{32,36}... | collective-permute-start | bytes 393224 | tf_op jit(solution)/shard_map/ppermute | solution.py:9
  237.2 79.6 %collective-permute-start.6 = (bf16[512,128]{1,0:T(8,128)(2,1)S(1)}, bf16[512,128]{1,0:T(8,128)(2,1)S(1)}, u32[]{:S(2)}, u32[]{:S(2)}) collective-permute-start(bf16[512,128]{1,0:T(8,128)(2,1)S(1)} %bitcast.58), channel_id=1, source_target_pairs={{0,252},{4,0},{8,4},{12,8},{16,12},{20,16},{24,20},{28,24},{32,28}... | collective-permute-start | bytes 393224 | tf_op jit(solution)/shard_map/ppermute | solution.py:9
  315.7 162.1 %collective-permute-start.5 = (bf16[512,128]{1,0:T(8,128)(2,1)S(1)}, bf16[512,128]{1,0:T(8,128)(2,1)S(1)}, u32[]{:S(2)}, u32[]{:S(2)}) collective-permute-start(bf16[512,128]{1,0:T(8,128)(2,1)S(1)} %fusion.6), channel_id=1, source_target_pairs={{0,4},{4,8},{8,12},{12,16},{16,20},{20,24},{24,28},{28,32},{32,36}... | collective-permute-start | bytes 393224 | tf_op jit(solution)/shard_map/ppermute | solution.py:9
  316.8 160.9 %collective-permute-start.7 = (bf16[512,128]{1,0:T(8,128)(2,1)S(1)}, bf16[512,128]{1,0:T(8,128)(2,1)S(1)}, u32[]{:S(2)}, u32[]{:S(2)}) collective-permute-start(bf16[512,128]{1,0:T(8,128)(2,1)S(1)} %fusion.5), channel_id=1, source_target_pairs={{0,252},{4,0},{8,4},{12,8},{16,12},{20,16},{24,20},{28,24},{32,28}... | collective-permute-start | bytes 393224 | tf_op jit(solution)/shard_map/ppermute | solution.py:9
Sparse Core Ops, SparseCore 0:
  130.8 18.3 reduce-scatter.1
  234.6 241.5 all-reduce.1
where the time goes:
time: 488 us; the launch traced here: 485 us
  waiting for transfers between devices  173 us (35%)
  other arithmetic  102 us (21%)
  blocking collectives  80.5 us (16%)
  local copies, waits for them, and re-layouts  48.9 us (10%)
  starting transfers between devices  33.5 us (7%)
  matrix products  33.1 us (7%)
  between operations  14.3 us (3%)
    psum x1, waiting for transfers between devices, local(): weight_sum, bias_sum = lax.psum((weight_part, bias_part), ('blk', 'col'))  153 us
    psum x1, blocking collectives, local(): weight_sum, bias_sum = lax.psum((weight_part, bias_part), ('blk', 'col'))  73 us
    scatter-add x1, other arithmetic, local(): jax.ops.segment_sum(products.reshape(-1, tile_size, features), dest_tiles...  47.9 us
    scatter-add x1, other arithmetic, local(): jax.ops.segment_sum(back_terms.reshape(-1, tile_size, features), target_i...  47.9 us
    ppermute x8, starting transfers between devices, from_behind(): lax.ppermute(value, axis, [(i, (i + by) % length) for i in range(length)])  33.4 us
    reduce_scatter x1, waiting for transfers between devices, local(): sums = lax.psum_scatter(block_sums, 'col', scatter_dimension=0, tiled=True)  18.1 us
    reshape x1, local copies, waits for them, and re-layouts, local(): adjacency.reshape(offset_count, slot_count, tile_size, tile_size)  16.3 us
    dot_general x1, matrix products, local(): jnp.einsum('ksrq,ksrf->ksqf', adjacency, picked_grad, preferred_element_t...  15.2 us
  transfers between devices with their start and end apart: 10, of which 3 were waited for; matrix products, arithmetic and copies ran while one was open for 7% of the time, Pallas kernels for 0%

commit v1 on v0

v1 whole, which is shorter than its diff:
```python
import functools

import jax
import jax.numpy as jnp
from jax import lax
from jax.experimental import pallas as pl
from jax.experimental.pallas import tpu as pltpu
from jax.sharding import PartitionSpec as P

F32 = jnp.float32
BF16 = jnp.bfloat16
MESH = pl.DeviceIdType.MESH
COLS = 4
HI = 2
ZLEN = 8


def remote(src, dst, send_sem, recv_sem, blk, col):
    return pltpu.make_async_remote_copy(
        src_ref=src,
        dst_ref=dst,
        send_sem=send_sem,
        recv_sem=recv_sem,
        device_id={"blk": blk, "col": col},
        device_id_type=MESH,
    )


def loop(count, body):
    def step(i, carry):
        body(i)
        return carry

    lax.fori_loop(0, count, step, 0)


def kernel(
    n_blk,
    n_z,
    norm,
    prev,
    last,
    feats,
    deg,
    adj,
    weight,
    bias,
    cot,
    act_out,
    gf_out,
    gw_out,
    gb_out,
    tiles,
    chain,
    dense,
    feat_v,
    weight_v,
    cot_v,
    act_v,
    scale_col,
    source,
    own_sum,
    rs_send,
    rs_recv,
    hidden,
    back,
    back_send,
    back_recv,
    r1_send,
    r1_recv,
    r2_send,
    r2_recv,
    r3_recv,
    g1,
    g2,
    in_sem,
    tile_sem,
    act_sem,
    src_ss,
    src_rs,
    rs_ss,
    rs_rs,
    hid_ss,
    hid_rs,
    back_ss,
    back_rs,
    r1_ss,
    r1_rs,
    r2_ss,
    r2_rs,
    r3_ss,
    r3_rs,
    g1_ss,
    g1_rs,
    g2_ss,
    g2_rs,
):
    span, slots, tile, _ = tiles.shape
    reach = span // 2
    rows, fin = feats.shape
    dev_tiles = rows // tile
    block_tiles = COLS * dev_tiles
    n_xy = n_blk // n_z

    blk = lax.axis_index("blk")
    col = lax.axis_index("col")
    hi = blk % HI
    z = (blk // HI) % n_z
    xy = (blk // (HI * n_z)) * HI + hi

    def block_at(z_, xy_):
        return ((xy_ // HI) * n_z + z_) * HI + xy_ % HI

    def near(k):
        return (blk + k - reach + n_blk) % n_blk

    mates = [(col + 2) % COLS, COLS - 1 - col, col + 1 - 2 * (col % 2)]

    copies_in = [
        pltpu.make_async_copy(feats, feat_v, in_sem.at[0]),
        pltpu.make_async_copy(weight, weight_v, in_sem.at[1]),
        pltpu.make_async_copy(cot, cot_v, in_sem.at[2]),
    ]
    copies_in[0].start()

    def tile_copy(k):
        return pltpu.make_async_copy(adj.at[pl.ds(k * slots, slots)], tiles.at[k], tile_sem.at[k])

    loop(span, lambda k: tile_copy(k).start())
    copies_in[1].start()
    copies_in[2].start()

    barrier = pltpu.get_barrier_semaphore()

    def hello(b, c):
        pl.semaphore_signal(barrier, inc=1, device_id={"blk": b, "col": c}, device_id_type=MESH)

    for k in range(span):
        if k != reach:
            hello(near(k), col)
    for mate in mates:
        hello(blk, mate)
    loop(n_z - 1, lambda i: hello(block_at((z + 1 + i) % n_z, xy), col))
    loop(n_xy - 1, lambda i: hello(block_at(z, (xy + 1 + i) % n_xy), col))

    scale_row = lax.rsqrt(deg[...].astype(F32))
    scale_col[...] = jnp.transpose(jnp.broadcast_to(scale_row, (fin, rows)))
    copies_in[0].wait()
    source[reach] = (scale_col[...] * feat_v[...].astype(F32)).astype(BF16)
    chain[slots] = jnp.zeros((tile, tile), F32)

    pl.semaphore_wait(barrier, (span - 1) + (COLS - 1) + (n_z - 1) + (n_xy - 1))

    sends = []
    for k in (1, 3, 0, 4):
        sends.append(
            remote(source.at[reach], source.at[k], src_ss.at[k], src_rs.at[k], near(span - 1 - k), col)
        )
        sends[-1].start()
    arrivals = list(sends)

    def build(k):
        tile_copy(k).wait()

        def slot(s):
            chain[s] = tiles[k, s].astype(F32) + chain[prev[k * slots + s]]

        loop(slots, slot)

        def row(r):
            cells = [
                chain[last[(k * block_tiles + r) * dev_tiles + c]].astype(BF16)
                for c in range(dev_tiles)
            ]
            dense[k, pl.ds(r * tile, tile), :] = jnp.concatenate(cells, axis=1)

        loop(block_tiles, row)

    loop(span, build)

    for copy in arrivals:
        copy.wait_recv()

    def chunk_sum(j):
        total = jnp.zeros((rows, fin), F32)
        for k in range(span):
            total += jnp.dot(
                dense[k, pl.ds(j * rows, rows), :], source[k], preferred_element_type=F32
            )
        return total

    rs_copies = []
    for d, mate in enumerate(mates):
        rs_send[d] = chunk_sum(mate).astype(BF16)
        copy = remote(rs_send.at[d], rs_recv.at[d], rs_ss.at[d], rs_rs.at[d], blk, mate)
        copy.start()
        rs_copies.append(copy)
    own_sum[...] = chunk_sum(col)
    copies_in[1].wait()
    copies_in[2].wait()
    sums = own_sum[...]
    for d in (2, 0, 1):
        rs_copies[d].wait_recv()
        sums = sums + rs_recv[d].astype(F32)
    sends += rs_copies

    agg = scale_col[...] * sums
    agg_t = jnp.transpose(agg).astype(BF16)
    agg = agg.astype(BF16)
    pre = jnp.dot(agg, weight_v[...], preferred_element_type=F32) + bias[...]
    gate = jax.nn.sigmoid(pre)
    grad_pre = cot_v[...].astype(F32) * gate * (1.0 + pre * (1.0 - gate))
    low = grad_pre.astype(BF16)
    hidden_t = lax.dot_general(
        weight_v[...], low, (((1,), (1,)), ((), ())), preferred_element_type=F32
    )
    hidden[col] = (hidden_t * scale_row).astype(BF16)
    hid_copies = []
    for d, mate in enumerate(mates):
        copy = remote(hidden.at[col], hidden.at[col], hid_ss.at[d], hid_rs.at[col], blk, mate)
        copy.start()
        sends.append(copy)

    def hidden_from(c):
        return remote(hidden.at[c], hidden.at[c], hid_ss.at[0], hid_rs.at[c], blk, c)

    act_v[...] = (pre * gate).astype(BF16)
    act_copy = pltpu.make_async_copy(act_v, act_out, act_sem)
    act_copy.start()

    part = jnp.dot(agg_t, low, preferred_element_type=F32)
    bias_part = jnp.sum(grad_pre, axis=0, keepdims=True)
    half = part.shape[0] // 2
    bias_rows = jnp.concatenate(
        [bias_part[:, :fin], bias_part[:, fin:], jnp.zeros((6, fin), F32)], axis=0
    )
    for c in range(COLS):
        r1_send[c, :half, :] = part[
            (c % 2) * half : (c % 2 + 1) * half, (c // 2) * fin : (c // 2 + 1) * fin
        ]
        r1_send[c, half:, :] = bias_rows
    r1_recv[col] = r1_send[col]
    for d, mate in enumerate(mates):
        copy = remote(r1_send.at[mate], r1_recv.at[col], r1_ss.at[d], r1_rs.at[col], blk, mate)
        copy.start()
        sends.append(copy)

    def back_term(k, c):
        return jnp.dot(
            hidden[c], dense[k, pl.ds(c * rows, rows), :], preferred_element_type=F32
        )

    def back_first(k):
        back[k] = back_term(k, col)

    loop(span, back_first)

    def back_more(c):
        hidden_from(c).wait_recv()

        def one(k):
            back[k] = back[k] + back_term(k, c)

        loop(span, one)

    back_more(mates[2])

    for mate in mates:
        remote(r1_send.at[mate], r1_recv.at[mate], r1_ss.at[0], r1_rs.at[mate], blk, mate).wait_recv()
    total = r1_recv[0] + r1_recv[1] + r1_recv[2] + r1_recv[3]
    piece = half // n_z
    for i in range(n_z):
        r2_send[i, :piece, :] = total[i * piece : (i + 1) * piece]
        r2_send[i, piece:, :] = total[half:]
    r2_recv[z] = r2_send[z]

    def r2_copy(i, mine):
        other = (z + 1 + i) % n_z
        return remote(
            r2_send.at[other],
            r2_recv.at[z if mine else other],
            r2_ss.at[i],
            r2_rs.at[z if mine else other],
            block_at(other, xy),
            col,
        )

    loop(n_z - 1, lambda i: r2_copy(i, True).start())

    back_more(mates[0])

    def r2_wait(i):
        r2_copy(i, False).wait_recv()

    loop(n_z - 1, r2_wait)
    total = r2_recv[0]
    for i in range(1, n_z):
        total = total + r2_recv[i]
    r3_recv[xy] = total

    def r3_copy(i, mine):
        other = (xy + 1 + i) % n_xy
        return remote(
            r3_recv.at[xy],
            r3_recv.at[xy if mine else other],
            r3_ss.at[i],
            r3_rs.at[xy if mine else other],
            block_at(z, other),
            col,
        )

    loop(n_xy - 1, lambda i: r3_copy(i, True).start())

    hidden_from(mates[1]).wait_recv()
    back_copies = []
    for k in (1, 3, 0, 4):
        back_send[k] = (back[k] + back_term(k, mates[1])).astype(BF16)
        copy = remote(
            back_send.at[k], back_recv.at[k], back_ss.at[k], back_rs.at[k], near(k), col
        )
        copy.start()
        back_copies.append(copy)
    own = back[reach] + back_term(reach, mates[1])
    sends += back_copies

    loop(n_xy - 1, lambda i: r3_copy(i, False).wait_recv())
    total = r3_recv[0]
    for i in range(1, n_xy):
        total = total + r3_recv[i]
    g1[z] = total[:piece] * norm
    gb_out[:, :fin] = total[piece : piece + 1] * norm
    gb_out[:, fin:] = total[piece + 1 : piece + 2] * norm

    def g1_copy(i, mine):
        other = (z + 1 + i) % n_z
        return remote(
            g1.at[z],
            g1.at[z if mine else other],
            g1_ss.at[i],
            g1_rs.at[z if mine else other],
            block_at(other, xy),
            col,
        )

    loop(n_z - 1, lambda i: g1_copy(i, True).start())
    back[reach] = own
    loop(n_z - 1, lambda i: g1_copy(i, False).wait_recv())
    g2[col] = jnp.concatenate([g1[i] for i in range(n_z)], axis=0)
    for d, mate in enumerate(mates):
        copy = remote(g2.at[col], g2.at[col], g2_ss.at[d], g2_rs.at[col], blk, mate)
        copy.start()
        sends.append(copy)

    total = back[reach]
    for copy, k in zip(back_copies, (1, 3, 0, 4), strict=True):
        copy.wait_recv()
        total = total + back_recv[k].astype(F32)
    gf_out[...] = jnp.transpose(total * scale_row).astype(BF16)

    for mate in mates:
        remote(g2.at[mate], g2.at[mate], g2_ss.at[0], g2_rs.at[mate], blk, mate).wait_recv()
    for c in range(COLS):
        gw_out[(c % 2) * half : (c % 2 + 1) * half, (c // 2) * fin : (c // 2 + 1) * fin] = g2[c]

    for copy in sends:
        copy.wait_send()
    loop(n_z - 1, lambda i: r2_copy(i, True).wait_send())
    loop(n_xy - 1, lambda i: r3_copy(i, True).wait_send())
    loop(n_z - 1, lambda i: g1_copy(i, True).wait_send())
    act_copy.wait()


def local(
    node_features, degree, adjacency, tile_rows, tile_cols, counts, weight, bias_vector, cotangent
):
    span = counts.shape[0]
    tile = adjacency.shape[1]
    slots = adjacency.shape[0] // span
    rows, fin = node_features.shape
    fh = weight.shape[1]
    dev_tiles = rows // tile
    n_cells = COLS * dev_tiles * dev_tiles
    n_blk = lax.axis_size("blk")
    n_z = min(ZLEN, n_blk // HI)
    n_xy = n_blk // n_z
    norm = float(rows * n_blk * COLS) ** (-0.5)

    cell = (tile_rows * dev_tiles + tile_cols).reshape(span, slots)
    index = jnp.arange(slots, dtype=jnp.int32)
    same = (cell[:, :, None] == cell[:, None, :]) & (index[None, None, :] < index[None, :, None])
    prev = jnp.max(jnp.where(same, index[None, None, :], -1), axis=2)
    prev = jnp.where(prev < 0, slots, prev).reshape(-1)
    hit = (jnp.arange(n_cells, dtype=jnp.int32)[None, :, None] == cell[:, None, :]) & (
        index[None, None, :] < counts[:, None, None]
    )
    last = jnp.max(jnp.where(hit, index[None, None, :], -1), axis=2)
    last = jnp.where(last < 0, slots, last).reshape(-1)

    half = fin // 2
    piece = half // n_z
    vmem = pltpu.VMEM
    dma = pltpu.SemaphoreType.DMA
    anywhere = pl.BlockSpec(memory_space=pl.ANY)
    in_vmem = pl.BlockSpec(memory_space=pltpu.VMEM)
    in_smem = pl.BlockSpec(memory_space=pltpu.SMEM)
    shape = jax.ShapeDtypeStruct
    act, gf, gw, gb = pl.pallas_call(
        functools.partial(kernel, n_blk, n_z, norm),
        out_shape=(
            shape((rows, fh), BF16),
            shape((rows, fin), BF16),
            shape((fin, fh), F32),
            shape((1, fh), F32),
        ),
        in_specs=[in_smem, in_smem, anywhere, in_vmem, anywhere, anywhere, in_vmem, anywhere],
        out_specs=(anywhere, in_vmem, in_vmem, in_vmem),
        scratch_shapes=[
            vmem((span, slots, tile, tile), BF16),
            vmem((slots + 1, tile, tile), F32),
            vmem((span, COLS * rows, rows), BF16),
            vmem((rows, fin), BF16),
            vmem((fin, fh), BF16),
            vmem((rows, fh), BF16),
            vmem((rows, fh), BF16),
            vmem((rows, fin), F32),
            vmem((span, rows, fin), BF16),
            vmem((rows, fin), F32),
            vmem((COLS - 1, rows, fin), BF16),
            vmem((COLS - 1, rows, fin), BF16),
            vmem((COLS, fin, rows), BF16),
            vmem((span, fin, rows), F32),
            vmem((span, fin, rows), BF16),
            vmem((span, fin, rows), BF16),
            vmem((COLS, half + 8, fin), F32),
            vmem((COLS, half + 8, fin), F32),
            vmem((n_z, piece + 8, fin), F32),
            vmem((n_z, piece + 8, fin), F32),
            vmem((n_xy, piece + 8, fin), F32),
            vmem((n_z, piece, fin), F32),
            vmem((COLS, half, fin), F32),
            dma((3,)),
            dma((span,)),
            dma,
            dma((span,)),
            dma((span,)),
            dma((COLS - 1,)),
            dma((COLS - 1,)),
            dma((COLS - 1,)),
            dma((COLS,)),
            dma((span,)),
            dma((span,)),
            dma((COLS - 1,)),
            dma((COLS,)),
            dma((n_z - 1,)),
            dma((n_z,)),
            dma((n_xy - 1,)),
            dma((n_xy,)),
            dma((n_z - 1,)),
            dma((n_z,)),
            dma((COLS - 1,)),
            dma((COLS,)),
        ],
        compiler_params=pltpu.CompilerParams(
            collective_id=0, has_side_effects=True, vmem_limit_bytes=52 * 2**20
        ),
        name="graph_layer",
    )(
        prev,
        last,
        node_features,
        degree.reshape(1, rows),
        adjacency,
        weight,
        bias_vector.reshape(1, fh),
        cotangent,
    )
    return act, gf, gw, gb.reshape(fh)


def solution(mesh):
    return jax.shard_map(
        local,
        mesh=mesh,
        in_specs=(
            P(("blk", "col"), None),
            P(("blk", "col")),
            P(("blk", "col"), None, None),
            P(("blk", "col")),
            P(("blk", "col")),
            P(("blk", "col")),
            P(),
            P(),
            P(("blk", "col"), None),
        ),
        out_specs=(P(("blk", "col"), None), P(("blk", "col"), None), P(), P()),
        check_vma=False,
    )
```

time: 488 us -> 65.7 us (0.13)
  waiting for transfers between devices: 173 us -> 0 us
  other arithmetic: 102 us -> 1.9 us
  blocking collectives: 80.5 us -> 0 us
  Pallas kernels: 0 us -> 56.1 us
  local copies, waits for them, and re-layouts: 48.9 us -> 6.87 us
  starting transfers between devices: 33.5 us -> 0 us
  matrix products: 33.1 us -> 0 us
  between operations: 14.3 us -> 0.66 us
    psum x1 -> x0, waiting for transfers between devices: 153 us -> none  [local(): weight_sum, bias_sum = lax.psum((weight_part, bias_part), ('blk', 'col'))]
    scatter-add x2 -> x0, other arithmetic: 95.8 us -> none  [the longest x1 47.9 us: local(): jax.ops.segment_sum(products.reshape(-1, tile_size, features), dest_tiles...]
    psum x1 -> x0, blocking collectives: 73 us -> none  [local(): weight_sum, bias_sum = lax.psum((weight_part, bias_part), ('blk', 'col'))]
    pallas_call x0 -> x1, Pallas kernels: none -> 56.1 us  [local(): pl.pallas_call(functools.partial(kernel, n_blk, n_z, norm), out_shape=(sh...]
    ppermute x8 -> x0, starting transfers between devices: 33.4 us -> none  [from_behind(): lax.ppermute(value, axis, [(i, (i + by) % length) for i in range(length)])]
    dot_general x5 -> x0, matrix products: 33.1 us -> none  [the longest x1 15.2 us: local(): jnp.einsum('ksrq,ksrf->ksqf', adjacency, picked_grad, preferred_element_t...]
    gather x6 -> x0, local copies, waits for them, and re-layouts: 20.4 us -> none  [the longest x1 11.1 us: local(): block_grad.reshape(block_tiles, tile_size, features)[dest_tiles]]
    reduce_scatter x1 -> x0, waiting for transfers between devices: 18.1 us -> none  [local(): sums = lax.psum_scatter(block_sums, 'col', scatter_dimension=0, tiled=True)]
  transfers between devices with their start and end apart: 10 -> 0, of which waited for: 3 -> 0; matrix products, arithmetic and copies ran while one was open for 7% -> 0% of each run, Pallas kernels for 0% -> 0%
where the time goes in v1:
time: 65.7 us; the launch traced here: 65.5 us
  Pallas kernels  56.1 us (85%)
  local copies, waits for them, and re-layouts  6.87 us (10%)
  other arithmetic  1.9 us (3%)
  between operations  0.66 us (1%)
    pallas_call x1, Pallas kernels, local(): pl.pallas_call(functools.partial(kernel, n_blk, n_z, norm), out_shape=(sh...  56.1 us
    unnamed x14, local copies, waits for them, and re-layouts  6.63 us

profile of v1, /device:TPU:1, one launch (start us, length us, event | category | flops | bytes accessed | tf_op | source)
XLA Modules:
  0.0 65.5 jit_solution(9542647557576252136)
XLA Ops:
  0.6 0.7 %iota_compare_fusion.2 = pred[5,72]{1,0:T(8,128)(4,1)S(1)} fusion(s32[5]{0:T(128)} %param.14), kind=kLoop, calls=%fused_computation.7 | loop fusion | flops 360 | bytes 380 | tf_op jit(solution)/shard_map/lt | solution.py:394
  1.4 0.7 %multiply_add_fusion = s32[360]{0:T(512)S(1)} fusion(s32[360]{0:T(512)} %param.13, s32[360]{0:T(512)} %param.12), kind=kLoop, calls=%fused_computation.8 | loop fusion | flops 720 | bytes 4320 | tf_op jit(solution)/shard_map/add | solution.py:388
  2.1 0.1 eq.28
  2.1 0.2 select_reduce_fusion.1
  2.3 0.1 reduce_max.25
  2.4 0.3 select_reduce_fusion
  2.7 0.1 reduce_max.23
  2.8 0.0 copy-start
  2.8 1.0 %copy-done = bf16[512,256]{1,0:T(8,128)(2,1)S(1)} copy-done((bf16[512,256]{1,0:T(8,128)(2,1)S(1)}, bf16[512,256]{1,0:T(8,128)(2,1)}, u32[]{:S(2)}) %copy-start) | copy-done | bytes 262168
  3.7 0.0 copy-start.1
  3.7 0.9 %copy-done.1 = bf16[512,128]{1,0:T(8,128)(2,1)S(1)} copy-done((bf16[512,128]{1,0:T(8,128)(2,1)S(1)}, bf16[512,128]{1,0:T(8,128)(2,1)}, u32[]{:S(2)}) %copy-start.1) | copy-done | bytes 131096
  4.6 0.0 copy-start.2
  4.6 0.8 %copy-done.2 = bf16[128,256]{1,0:T(8,128)(2,1)S(1)} copy-done((bf16[128,256]{1,0:T(8,128)(2,1)S(1)}, bf16[128,256]{1,0:T(8,128)(2,1)}, u32[]{:S(2)}) %copy-start.2) | copy-done | bytes 65560
  5.5 0.0 copy-start.3
  5.5 0.7 %copy-done.3 = s32[512]{0:T(512)S(1)} copy-done((s32[512]{0:T(512)S(1)}, s32[512]{0:T(512)}, u32[]{:S(2)}) %copy-start.3) | copy-done | bytes 2072
  6.2 0.0 copy-start.4
  6.2 0.7 %copy-done.4 = f32[256]{0:T(256)S(1)} copy-done((f32[256]{0:T(256)S(1)}, f32[256]{0:T(256)}, u32[]{:S(2)}) %copy-start.4) | copy-done | bytes 1048
  6.8 56.1 %graph_layer.1 = (bf16[512,256]{1,0:T(8,128)(2,1)S(1)}, bf16[512,128]{1,0:T(8,128)(2,1)S(1)}, f32[128,256]{1,0:T(8,128)S(1)}, f32[1,256]{1,0:T(1,128)S(1)}) custom-call(s32[360]{0:T(512)S(1)} %compare_select_fusion.1.prev, s32[320]{0:T(512)S(1)} %compare_select_fusion.last, bf16[512,128]{1,0:T(8,128)(2,1)S(1)} %copy-done.1, s32[1,512]{1,0:T(1,128)S(1)} %bitcast.3, ...), custom_call_target="tpu_custom_call" | custom-call | tf_op jit(solution)/shard_map/graph_layer/pallas_call | solution.py:407
  62.9 0.7 %copy.17 = bf16[512,256]{1,0:T(8,128)(2,1)} copy(bf16[512,256]{1,0:T(8,128)(2,1)S(1)} %get-tuple-element.16) | data formatting | bytes 524288
  63.6 0.7 copy.18
  64.3 0.7 copy.19
  64.9 0.6 copy.20
  (3 shorter events, 0.0 us)
Async XLA Ops:
  2.8 1.0 %copy-start = (bf16[512,256]{1,0:T(8,128)(2,1)S(1)}, bf16[512,256]{1,0:T(8,128)(2,1)}, u32[]{:S(2)}) copy-start(bf16[512,256]{1,0:T(8,128)(2,1)} %cot.1) | copy-start | bytes 786436
  3.7 0.9 %copy-start.1 = (bf16[512,128]{1,0:T(8,128)(2,1)S(1)}, bf16[512,128]{1,0:T(8,128)(2,1)}, u32[]{:S(2)}) copy-start(bf16[512,128]{1,0:T(8,128)(2,1)} %feats.1) | copy-start | bytes 393220
  4.6 0.8 %copy-start.2 = (bf16[128,256]{1,0:T(8,128)(2,1)S(1)}, bf16[128,256]{1,0:T(8,128)(2,1)}, u32[]{:S(2)}) copy-start(bf16[128,256]{1,0:T(8,128)(2,1)} %weight.1) | copy-start | bytes 196612
  5.5 0.7 %copy-start.3 = (s32[512]{0:T(512)S(1)}, s32[512]{0:T(512)}, u32[]{:S(2)}) copy-start(s32[512]{0:T(512)} %param.10) | copy-start | bytes 6148
  6.2 0.7 %copy-start.4 = (f32[256]{0:T(256)S(1)}, f32[256]{0:T(256)}, u32[]{:S(2)}) copy-start(f32[256]{0:T(256)} %param.16) | copy-start | bytes 3076

commit v2 on v1

v2 whole, which is shorter than its diff:
```python
import functools

import jax
import jax.numpy as jnp
from jax import lax
from jax.experimental import pallas as pl
from jax.experimental.pallas import tpu as pltpu
from jax.sharding import PartitionSpec as P

F32 = jnp.float32
BF16 = jnp.bfloat16
MESH = pl.DeviceIdType.MESH
COLS = 4
HI = 2
ZLEN = 8


def remote(src, dst, send_sem, recv_sem, blk, col):
    return pltpu.make_async_remote_copy(
        src_ref=src,
        dst_ref=dst,
        send_sem=send_sem,
        recv_sem=recv_sem,
        device_id={"blk": blk, "col": col},
        device_id_type=MESH,
    )


def loop(count, body):
    def step(i, carry):
        body(i)
        return carry

    lax.fori_loop(0, count, step, 0)


def kernel(
    n_blk,
    n_z,
    norm,
    tile_rows,
    tile_cols,
    counts,
    feats,
    deg,
    adj,
    weight,
    bias,
    cot,
    act_out,
    gf_out,
    gw_out,
    gb_out,
    tiles,
    chain,
    dense,
    feat_v,
    deg_v,
    weight_v,
    bias_v,
    cot_v,
    rows_v,
    cols_v,
    keys_v,
    index_v,
    counts_s,
    index_s,
    scale_col,
    source,
    own_sum,
    rs_send,
    rs_recv,
    hidden,
    back,
    back_send,
    back_recv,
    r1_send,
    r1_recv,
    r2_send,
    r2_recv,
    r3_recv,
    g1,
    g2,
    in_sem,
    tile_sem,
    index_sem,
    src_ss,
    src_rs,
    rs_ss,
    rs_rs,
    hid_ss,
    hid_rs,
    back_ss,
    back_rs,
    r1_ss,
    r1_rs,
    r2_ss,
    r2_rs,
    r3_ss,
    r3_rs,
    g1_ss,
    g1_rs,
    g2_ss,
    g2_rs,
):
    span, slots, tile, _ = tiles.shape
    reach = span // 2
    rows, fin = feats.shape
    dev_tiles = rows // tile
    block_tiles = COLS * dev_tiles
    n_cells = block_tiles * dev_tiles
    n_xy = n_blk // n_z
    n_x = n_xy // HI
    padded = keys_v.shape[1]

    blk = lax.axis_index("blk")
    col = lax.axis_index("col")
    hi = blk % HI
    z = (blk // HI) % n_z
    x = blk // (HI * n_z)
    xy = x * HI + hi

    def near(k):
        return (blk + k - reach + n_blk) % n_blk

    over, across, twin = (col + 2) % COLS, COLS - 1 - col, col + 1 - 2 * (col % 2)
    mates = [over, across, twin]

    def ring(step, length):
        return min(step, length - step)

    z_steps = sorted(range(1, n_z), key=lambda s: -ring(s, n_z))
    z_mates = [((z + s) % n_z, (x * n_z + (z + s) % n_z) * HI + hi) for s in z_steps]
    xy_steps = [(a, b) for a in range(n_x) for b in range(HI) if (a, b) != (0, 0)]
    xy_steps.sort(key=lambda s: -ring(s[0], n_x) - 2 * s[1])
    xy_mates = []
    for a, b in xy_steps:
        x_to, hi_to = (x + a) % n_x, (hi + b) % HI
        xy_mates.append((x_to * HI + hi_to, (x_to * n_z + z) * HI + hi_to))

    loads = [
        pltpu.make_async_copy(src, dst, in_sem.at[i])
        for i, (src, dst) in enumerate(
            (
                (deg, deg_v),
                (feats, feat_v),
                (tile_rows, rows_v),
                (tile_cols, cols_v),
                (counts, counts_s),
                (weight, weight_v),
                (bias, bias_v),
                (cot, cot_v),
            )
        )
    ]
    for load in loads[:5]:
        load.start()

    barrier = pltpu.get_barrier_semaphore()

    def hello(b, c):
        pl.semaphore_signal(barrier, inc=1, device_id={"blk": b, "col": c}, device_id_type=MESH)

    for k in (1, 3, 0, 4):
        hello(near(k), col)
    for mate in mates:
        hello(blk, mate)
    for _, other in xy_mates + z_mates:
        hello(other, col)

    def tile_copy(k):
        return pltpu.make_async_copy(adj.at[pl.ds(k * slots, slots)], tiles.at[k], tile_sem.at[k])

    loop(span, lambda k: tile_copy(k).start())

    loads[0].wait()
    scale_row = lax.rsqrt(deg_v[...].astype(F32))
    scale_col[...] = jnp.transpose(jnp.broadcast_to(scale_row, (fin, rows)))
    loads[1].wait()
    source[reach] = (scale_col[...] * feat_v[...].astype(F32)).astype(BF16)

    pl.semaphore_wait(barrier, (span - 1) + (COLS - 1) + len(xy_mates) + len(z_mates))

    sends = []
    for k in (1, 3, 0, 4):
        sends.append(
            remote(source.at[reach], source.at[k], src_ss.at[k], src_rs.at[k], near(span - 1 - k), col)
        )
        sends[-1].start()
    arrivals = list(sends)
    for load in loads[5:]:
        load.start()

    for load in loads[2:5]:
        load.wait()

    def place(lane, size):
        group = jnp.zeros_like(lane)
        for g in range(1, span):
            group += (lane >= g * size).astype(jnp.int32)
        return group

    cell = (rows_v[...] * dev_tiles + cols_v[...]).reshape(1, span * slots)
    lane = lax.broadcasted_iota(jnp.int32, cell.shape, 1)
    group = place(lane, slots)
    limit = jnp.zeros_like(lane)
    for g in range(span):
        limit = jnp.where(group == g, counts_s[g], limit)
    keys = jnp.where(lane - group * slots < limit, group * n_cells + cell, -1 - group)
    keys_v[...] = jnp.full(keys_v.shape, -1 - span, jnp.int32)
    keys_v[:, : span * slots] = keys
    key_col = jnp.transpose(jnp.broadcast_to(keys_v[...], (128, padded)))
    at = lax.broadcasted_iota(jnp.int32, key_col.shape, 0)
    for b in range(padded // 128):
        lane = lax.broadcasted_iota(jnp.int32, (1, 128), 1) + b * 128
        hit = (key_col == keys_v[:, b * 128 : (b + 1) * 128]) & (at < lane)
        found = jnp.max(jnp.where(hit, at, -1), axis=0, keepdims=True)
        index_v[:, b * 128 : (b + 1) * 128] = jnp.where(
            found < 0, slots, found - place(lane, slots) * slots
        )
        found = jnp.max(jnp.where(key_col == lane, at, -1), axis=0, keepdims=True)
        index_v[:, padded + b * 128 : padded + (b + 1) * 128] = jnp.where(
            found < 0, slots, found - place(lane, n_cells) * slots
        )
    index_copy = pltpu.make_async_copy(index_v, index_s, index_sem)
    index_copy.start()
    chain[slots] = jnp.zeros((tile, tile), F32)
    index_copy.wait()

    def build(k):
        tile_copy(k).wait()

        def slot(s):
            chain[s] = tiles[k, s].astype(F32) + chain[index_s[0, k * slots + s]]

        loop(slots, slot)

        def row(r):
            cells = [
                chain[index_s[0, padded + (k * block_tiles + r) * dev_tiles + c]].astype(BF16)
                for c in range(dev_tiles)
            ]
            dense[k, pl.ds(r * tile, tile), :] = jnp.concatenate(cells, axis=1)

        loop(block_tiles, row)

    loop(span, build)

    for copy in arrivals:
        copy.wait_recv()

    def chunk_sum(j):
        total = jnp.zeros((rows, fin), F32)
        for k in range(span):
            total += jnp.dot(
                dense[k, pl.ds(j * rows, rows), :], source[k], preferred_element_type=F32
            )
        return total

    def rs_copy(i, mate):
        copy = remote(rs_send.at[i], rs_recv.at[i], rs_ss.at[i], rs_rs.at[i], blk, mate)
        copy.start()
        sends.append(copy)
        return copy

    rs_send[0] = chunk_sum(across).astype(BF16)
    first = rs_copy(0, twin)
    partial = chunk_sum(over)
    first.wait_recv()
    rs_send[2] = (partial + rs_recv[0].astype(F32)).astype(BF16)
    third = rs_copy(2, over)
    rs_send[1] = chunk_sum(twin).astype(BF16)
    second = rs_copy(1, twin)
    own_sum[...] = chunk_sum(col)
    for load in loads[5:]:
        load.wait()
    second.wait_recv()
    own_sum[...] = own_sum[...] + rs_recv[1].astype(F32)
    third.wait_recv()
    sums = own_sum[...] + rs_recv[2].astype(F32)

    agg = scale_col[...] * sums
    agg_t = jnp.transpose(agg).astype(BF16)
    agg = agg.astype(BF16)
    pre = jnp.dot(agg, weight_v[...], preferred_element_type=F32) + bias_v[...]
    gate = jax.nn.sigmoid(pre)
    grad_pre = cot_v[...].astype(F32) * gate * (1.0 + pre * (1.0 - gate))
    low = grad_pre.astype(BF16)
    act_out[...] = (pre * gate).astype(BF16)

    part = jnp.dot(agg_t, low, preferred_element_type=F32)
    bias_part = jnp.sum(grad_pre, axis=0, keepdims=True)
    half = part.shape[0] // 2
    bias_rows = jnp.concatenate(
        [bias_part[:, :fin], bias_part[:, fin:], jnp.zeros((6, fin), F32)], axis=0
    )
    for c in range(COLS):
        r1_send[c, :half, :] = part[
            (c % 2) * half : (c % 2 + 1) * half, (c // 2) * fin : (c // 2 + 1) * fin
        ]
        r1_send[c, half:, :] = bias_rows
    r1_recv[col] = r1_send[col]
    for d, mate in enumerate(mates):
        copy = remote(r1_send.at[mate], r1_recv.at[col], r1_ss.at[d], r1_rs.at[col], blk, mate)
        copy.start()
        sends.append(copy)

    hidden_t = lax.dot_general(
        weight_v[...], low, (((1,), (1,)), ((), ())), preferred_element_type=F32
    )
    scale_row = lax.rsqrt(deg_v[...].astype(F32))
    hidden[col] = (hidden_t * scale_row).astype(BF16)

    def hidden_copy(i, c, mate):
        return remote(hidden.at[c], hidden.at[c], hid_ss.at[i], hid_rs.at[c], blk, mate)

    def hidden_send(i, c, mate):
        copy = hidden_copy(i, c, mate)
        copy.start()
        sends.append(copy)

    hidden_send(0, col, over)
    hidden_send(1, col, twin)

    def back_term(k, c):
        return jnp.dot(
            hidden[c], dense[k, pl.ds(c * rows, rows), :], preferred_element_type=F32
        )

    def back_first(k):
        back[k] = back_term(k, col)

    loop(span, back_first)

    def back_more(c):
        def one(k):
            back[k] = back[k] + back_term(k, c)

        loop(span, one)

    hidden_copy(0, twin, twin).wait_recv()
    back_more(twin)

    for mate in mates:
        remote(r1_send.at[mate], r1_recv.at[mate], r1_ss.at[0], r1_rs.at[mate], blk, mate).wait_recv()
    total = r1_recv[0] + r1_recv[1] + r1_recv[2] + r1_recv[3]
    piece = half // n_xy
    for i in range(n_xy):
        r2_send[i, :piece, :] = total[i * piece : (i + 1) * piece]
        r2_send[i, piece:, :] = total[half:]
    r2_recv[xy] = r2_send[xy]
    for i, (to, other) in enumerate(xy_mates):
        copy = remote(r2_send.at[to], r2_recv.at[xy], r2_ss.at[i], r2_rs.at[xy], other, col)
        copy.start()
        sends.append(copy)

    hidden_copy(0, over, over).wait_recv()
    hidden_send(2, over, twin)
    back_more(over)

    hidden_copy(0, across, across).wait_recv()
    back_copies = []
    for k in (1, 3, 0, 4):
        back_send[k] = (back[k] + back_term(k, across)).astype(BF16)
        copy = remote(
            back_send.at[k], back_recv.at[k], back_ss.at[k], back_rs.at[k], near(k), col
        )
        copy.start()
        back_copies.append(copy)
    sends += back_copies

    for to, other in xy_mates:
        remote(r2_send.at[to], r2_recv.at[to], r2_ss.at[0], r2_rs.at[to], other, col).wait_recv()
    total = r2_recv[0]
    for i in range(1, n_xy):
        total = total + r2_recv[i]
    r3_recv[z] = total
    for i, (to, other) in enumerate(z_mates):
        copy = remote(r3_recv.at[z], r3_recv.at[z], r3_ss.at[i], r3_rs.at[z], other, col)
        copy.start()
        sends.append(copy)

    back[reach] = back[reach] + back_term(reach, across)

    for to, other in z_mates:
        remote(r3_recv.at[to], r3_recv.at[to], r3_ss.at[0], r3_rs.at[to], other, col).wait_recv()
    total = r3_recv[0]
    for i in range(1, n_z):
        total = total + r3_recv[i]
    g1[xy] = total[:piece] * norm
    for i, (to, other) in enumerate(xy_mates):
        copy = remote(g1.at[xy], g1.at[xy], g1_ss.at[i], g1_rs.at[xy], other, col)
        copy.start()
        sends.append(copy)
    gb_out[:, :fin] = total[piece : piece + 1] * norm
    gb_out[:, fin:] = total[piece + 1 : piece + 2] * norm

    def finish_back():
        total = back[reach]
        for copy, k in zip(back_copies, (1, 3, 0, 4), strict=True):
            copy.wait_recv()
            total = total + back_recv[k].astype(F32)
        gf_out[...] = jnp.transpose(total * lax.rsqrt(deg_v[...].astype(F32))).astype(BF16)

    for to, other in xy_mates:
        remote(g1.at[to], g1.at[to], g1_ss.at[0], g1_rs.at[to], other, col).wait_recv()
    g2[col] = jnp.concatenate([g1[i] for i in range(n_xy)], axis=0)
    for d, mate in enumerate(mates):
        copy = remote(g2.at[col], g2.at[col], g2_ss.at[d], g2_rs.at[col], blk, mate)
        copy.start()
        sends.append(copy)

    finish_back()

    for mate in mates:
        remote(g2.at[mate], g2.at[mate], g2_ss.at[0], g2_rs.at[mate], blk, mate).wait_recv()
    for c in range(COLS):
        gw_out[(c % 2) * half : (c % 2 + 1) * half, (c // 2) * fin : (c // 2 + 1) * fin] = g2[c]

    for copy in sends:
        copy.wait_send()


def deliver(*refs):
    sources, results, sems = refs[:4], refs[4:8], refs[8]
    copies = [
        pltpu.make_async_copy(a, b, sems.at[i])
        for i, (a, b) in enumerate(zip(sources, results, strict=True))
    ]
    for copy in copies:
        copy.start()
    for copy in copies:
        copy.wait()


def local(
    node_features, degree, adjacency, tile_rows, tile_cols, counts, weight, bias_vector, cotangent
):
    span = counts.shape[0]
    tile = adjacency.shape[1]
    slots = adjacency.shape[0] // span
    rows, fin = node_features.shape
    fh = weight.shape[1]
    dev_tiles = rows // tile
    n_cells = COLS * dev_tiles * dev_tiles
    n_blk = lax.axis_size("blk")
    n_z = min(ZLEN, n_blk // HI)
    n_xy = n_blk // n_z
    norm = float(rows * n_blk * COLS) ** (-0.5)
    padded = -(-span * max(slots, n_cells) // 128) * 128

    half = fin // 2
    piece = half // n_xy
    vmem = pltpu.VMEM
    dma = pltpu.SemaphoreType.DMA
    anywhere = pl.BlockSpec(memory_space=pl.ANY)
    in_vmem = pl.BlockSpec(memory_space=pltpu.VMEM)
    shape = jax.ShapeDtypeStruct
    out_shape = (
        shape((rows, fh), BF16),
        shape((rows, fin), BF16),
        shape((fin, fh), F32),
        shape((1, fh), F32),
    )
    inputs = (
        tile_rows,
        tile_cols,
        counts,
        node_features,
        degree.reshape(1, rows),
        adjacency,
        weight,
        bias_vector.reshape(1, fh),
        cotangent,
    )
    results = pl.pallas_call(
        functools.partial(kernel, n_blk, n_z, norm),
        out_shape=out_shape,
        in_specs=[anywhere] * len(inputs),
        out_specs=(in_vmem,) * 4,
        scratch_shapes=[
            vmem((span, slots, tile, tile), BF16),
            vmem((slots + 1, tile, tile), F32),
            vmem((span, COLS * rows, rows), BF16),
            vmem((rows, fin), BF16),
            vmem((1, rows), jnp.int32),
            vmem((fin, fh), BF16),
            vmem((1, fh), F32),
            vmem((rows, fh), BF16),
            vmem((span * slots,), jnp.int32),
            vmem((span * slots,), jnp.int32),
            vmem((1, padded), jnp.int32),
            vmem((1, 2 * padded), jnp.int32),
            pltpu.SMEM((span,), jnp.int32),
            pltpu.SMEM((1, 2 * padded), jnp.int32),
            vmem((rows, fin), F32),
            vmem((span, rows, fin), BF16),
            vmem((rows, fin), F32),
            vmem((3, rows, fin), BF16),
            vmem((3, rows, fin), BF16),
            vmem((COLS, fin, rows), BF16),
            vmem((span, fin, rows), F32),
            vmem((span, fin, rows), BF16),
            vmem((span, fin, rows), BF16),
            vmem((COLS, half + 8, fin), F32),
            vmem((COLS, half + 8, fin), F32),
            vmem((n_xy, piece + 8, fin), F32),
            vmem((n_xy, piece + 8, fin), F32),
            vmem((n_z, piece + 8, fin), F32),
            vmem((n_xy, piece, fin), F32),
            vmem((COLS, half, fin), F32),
            dma((8,)),
            dma((span,)),
            dma,
            dma((span,)),
            dma((span,)),
            dma((3,)),
            dma((3,)),
            dma((3,)),
            dma((COLS,)),
            dma((span,)),
            dma((span,)),
            dma((3,)),
            dma((COLS,)),
            dma((n_xy - 1,)),
            dma((n_xy,)),
            dma((n_z - 1,)),
            dma((n_z,)),
            dma((n_xy - 1,)),
            dma((n_xy,)),
            dma((3,)),
            dma((COLS,)),
        ],
        compiler_params=pltpu.CompilerParams(
            collective_id=0, has_side_effects=True, vmem_limit_bytes=52 * 2**20
        ),
        name="graph_layer",
    )(*(pltpu.with_memory_space_constraint(value, pltpu.HBM) for value in inputs))
    act, gf, gw, gb = pl.pallas_call(
        deliver,
        out_shape=out_shape,
        in_specs=[anywhere] * 4,
        out_specs=(anywhere,) * 4,
        scratch_shapes=[dma((4,))],
        name="graph_results",
    )(*(pltpu.with_memory_space_constraint(value, pltpu.VMEM) for value in results))
    return act, gf, gw, gb.reshape(fh)


def solution(mesh):
    return jax.shard_map(
        local,
        mesh=mesh,
        in_specs=(
            P(("blk", "col"), None),
            P(("blk", "col")),
            P(("blk", "col"), None, None),
            P(("blk", "col")),
            P(("blk", "col")),
            P(("blk", "col")),
            P(),
            P(),
            P(("blk", "col"), None),
        ),
        out_specs=(P(("blk", "col"), None), P(("blk", "col"), None), P(), P()),
        check_vma=False,
    )
```

time: 65.7 us -> 55.4 us (0.84)
  local copies, waits for them, and re-layouts: 6.87 us -> 0 us
  other arithmetic: 1.9 us -> 0 us
  Pallas kernels: 56.1 us -> 54.7 us
    unnamed x14 -> x0, local copies, waits for them, and re-layouts: 6.63 us -> none
    pallas_call x1 -> x2, Pallas kernels: 56.1 us -> 54.7 us  [the longest x1 53.9 us: local(): pl.pallas_call(functools.partial(kernel, n_blk, n_z, norm), out_shape=out...]
    lt x2 -> x0, other arithmetic: 0.74 us -> none  [the longest x1 0.73 us: local(): index[None, None, :] < counts[:, None, None]]
    add x1 -> x0, other arithmetic: 0.7 us -> none  [local(): cell = (tile_rows * dev_tiles + tile_cols).reshape(span, slots)]
where the time goes in v2:
time: 55.4 us; the launch traced here: 55.3 us
  Pallas kernels  54.7 us (99%)
  between operations  0.64 us (1%)
    pallas_call x1, Pallas kernels, local(): pl.pallas_call(functools.partial(kernel, n_blk, n_z, norm), out_shape=out...  53.9 us

profile of v2, /device:TPU:1, one launch (start us, length us, event | category | flops | bytes accessed | tf_op | source)
XLA Modules:
  0.0 55.3 jit_solution(2659536946114457486)
XLA Ops:
  0.6 53.9 %graph_layer.1 = (bf16[512,256]{1,0:T(8,128)(2,1)S(1)}, bf16[512,128]{1,0:T(8,128)(2,1)S(1)}, f32[128,256]{1,0:T(8,128)S(1)}, f32[1,256]{1,0:T(1,128)S(1)}) custom-call(s32[360]{0:T(512)} %tile_rows.1, s32[360]{0:T(512)} %tile_cols.1, s32[5]{0:T(128)} %counts.1, bf16[512,128]{1,0:T(8,128)(2,1)} %feats.1, s32[1,512]{1,0:T(1,128)} %bitcast.3, ...), custom_call_target="tpu_custom_call" | custom-call | tf_op jit(solution)/shard_map/graph_layer/pallas_call | solution.py:476
  54.5 0.8 %graph_results.1 = (bf16[512,256]{1,0:T(8,128)(2,1)}, bf16[512,128]{1,0:T(8,128)(2,1)}, f32[128,256]{1,0:T(8,128)}, f32[1,256]{1,0:T(1,128)}) custom-call(bf16[512,256]{1,0:T(8,128)(2,1)S(1)} %get-tuple-element.12.refs_0_, bf16[512,128]{1,0:T(8,128)(2,1)S(1)} %get-tuple-element.13.refs_1_, f32[128,256]{1,0:T(8,128)S(1)} %get-tuple-element.14.refs_2_, ...), custom_call_target="tpu_custom_call" | custom-call | tf_op jit(solution)/shard_map/graph_results/pallas_call | solution.py:539

commit v3 on v2

--- a/solution.py
+++ b/solution.py
@@ -79,7 +79,6 @@
     r2_send,
     r2_recv,
     r3_recv,
-    g1,
     g2,
     in_sem,
     tile_sem,
@@ -137,6 +136,7 @@
     for a, b in xy_steps:
         x_to, hi_to = (x + a) % n_x, (hi + b) % HI
         xy_mates.append((x_to * HI + hi_to, (x_to * n_z + z) * HI + hi_to))
+    plane = [(c, to, other) for to, other in xy_mates for c in (col, over)] + [(over, xy, blk)]
 
     loads = [
         pltpu.make_async_copy(src, dst, in_sem.at[i])
@@ -165,7 +165,10 @@
         hello(near(k), col)
     for mate in mates:
         hello(blk, mate)
-    for _, other in xy_mates + z_mates:
+    for _, other in xy_mates:
+        hello(other, col)
+        hello(other, over)
+    for _, other in z_mates:
         hello(other, col)
 
     def tile_copy(k):
@@ -179,7 +182,7 @@
     loads[1].wait()
     source[reach] = (scale_col[...] * feat_v[...].astype(F32)).astype(BF16)
 
-    pl.semaphore_wait(barrier, (span - 1) + (COLS - 1) + len(xy_mates) + len(z_mates))
+    pl.semaphore_wait(barrier, (span - 1) + (COLS - 1) + 2 * len(xy_mates) + len(z_mates))
 
     sends = []
     for k in (1, 3, 0, 4):
@@ -249,47 +252,78 @@
     for copy in arrivals:
         copy.wait_recv()
 
-    def chunk_sum(j):
-        total = jnp.zeros((rows, fin), F32)
+    side = rows // 2
+
+    def chunk_sum(j, h):
+        total = jnp.zeros((side, fin), F32)
         for k in range(span):
             total += jnp.dot(
-                dense[k, pl.ds(j * rows, rows), :], source[k], preferred_element_type=F32
+                dense[k, pl.ds(j * rows + h * side, side), :],
+                source[k],
+                preferred_element_type=F32,
             )
         return total
 
-    def rs_copy(i, mate):
-        copy = remote(rs_send.at[i], rs_recv.at[i], rs_ss.at[i], rs_rs.at[i], blk, mate)
+    def rs_copy(i, h, mate):
+        copy = remote(rs_send.at[i, h], rs_recv.at[i, h], rs_ss.at[i, h], rs_rs.at[i, h], blk, mate)
         copy.start()
         sends.append(copy)
         return copy
 
-    rs_send[0] = chunk_sum(across).astype(BF16)
-    first = rs_copy(0, twin)
-    partial = chunk_sum(over)
-    first.wait_recv()
-    rs_send[2] = (partial + rs_recv[0].astype(F32)).astype(BF16)
-    third = rs_copy(2, over)
-    rs_send[1] = chunk_sum(twin).astype(BF16)
-    second = rs_copy(1, twin)
-    own_sum[...] = chunk_sum(col)
+    first, second, third = [], [], []
+    for h in range(2):
+        rs_send[0, h] = chunk_sum(across, h).astype(BF16)
+        first.append(rs_copy(0, h, twin))
+    for h in range(2):
+        partial = chunk_sum(over, h)
+        first[h].wait_recv()
+        rs_send[2, h] = (partial + rs_recv[0, h].astype(F32)).astype(BF16)
+        third.append(rs_copy(2, h, over))
+    for h in range(2):
+        rs_send[1, h] = chunk_sum(twin, h).astype(BF16)
+        second.append(rs_copy(1, h, twin))
+    for h in range(2):
+        own_sum[h] = chunk_sum(col, h)
     for load in loads[5:]:
         load.wait()
-    second.wait_recv()
-    own_sum[...] = own_sum[...] + rs_recv[1].astype(F32)
-    third.wait_recv()
-    sums = own_sum[...] + rs_recv[2].astype(F32)
-
-    agg = scale_col[...] * sums
-    agg_t = jnp.transpose(agg).astype(BF16)
-    agg = agg.astype(BF16)
-    pre = jnp.dot(agg, weight_v[...], preferred_element_type=F32) + bias_v[...]
-    gate = jax.nn.sigmoid(pre)
-    grad_pre = cot_v[...].astype(F32) * gate * (1.0 + pre * (1.0 - gate))
-    low = grad_pre.astype(BF16)
-    act_out[...] = (pre * gate).astype(BF16)
-
-    part = jnp.dot(agg_t, low, preferred_element_type=F32)
-    bias_part = jnp.sum(grad_pre, axis=0, keepdims=True)
+    for h in range(2):
+        second[h].wait_recv()
+        own_sum[h] = own_sum[h] + rs_recv[1, h].astype(F32)
+
+    def hidden_copy(i, c, h, mate):
+        return remote(
+            hidden.at[c, h], hidden.at[c, h], hid_ss.at[i, h], hid_rs.at[c, h], blk, mate
+        )
+
+    def hidden_send(i, c, h, mate):
+        copy = hidden_copy(i, c, h, mate)
+        copy.start()
+        sends.append(copy)
+
+    part = jnp.zeros((fin, weight_v.shape[1]), F32)
+    bias_part = jnp.zeros((1, weight_v.shape[1]), F32)
+    for h in range(2):
+        third[h].wait_recv()
+        sums = own_sum[h] + rs_recv[2, h].astype(F32)
+        agg = scale_col[h * side : (h + 1) * side] * sums
+        agg_t = jnp.transpose(agg).astype(BF16)
+        agg = agg.astype(BF16)
+        pre = jnp.dot(agg, weight_v[...], preferred_element_type=F32) + bias_v[...]
+        gate = jax.nn.sigmoid(pre)
+        cot_h = cot_v[h * side : (h + 1) * side].astype(F32)
+        grad_pre = cot_h * gate * (1.0 + pre * (1.0 - gate))
+        low = grad_pre.astype(BF16)
+        hidden_t = lax.dot_general(
+            weight_v[...], low, (((1,), (1,)), ((), ())), preferred_element_type=F32
+        )
+        scale_row = lax.rsqrt(deg_v[:, h * side : (h + 1) * side].astype(F32))
+        hidden[col, h] = (hidden_t * scale_row).astype(BF16)
+        hidden_send(0, col, h, over)
+        hidden_send(1, col, h, twin)
+        act_out[h * side : (h + 1) * side] = (pre * gate).astype(BF16)
+        part += jnp.dot(agg_t, low, preferred_element_type=F32)
+        bias_part += jnp.sum(grad_pre, axis=0, keepdims=True)
+
     half = part.shape[0] // 2
     bias_rows = jnp.concatenate(
         [bias_part[:, :fin], bias_part[:, fin:], jnp.zeros((6, fin), F32)], axis=0
@@ -299,38 +333,20 @@
             (c % 2) * half : (c % 2 + 1) * half, (c // 2) * fin : (c // 2 + 1) * fin
         ]
         r1_send[c, half:, :] = bias_rows
-    r1_recv[col] = r1_send[col]
-    for d, mate in enumerate(mates):
-        copy = remote(r1_send.at[mate], r1_recv.at[col], r1_ss.at[d], r1_rs.at[col], blk, mate)
+    for i, c in enumerate((across, twin)):
+        copy = remote(r1_send.at[c], r1_recv.at[c], r1_ss.at[i], r1_rs.at[c // 2], blk, twin)
         copy.start()
         sends.append(copy)
 
-    hidden_t = lax.dot_general(
-        weight_v[...], low, (((1,), (1,)), ((), ())), preferred_element_type=F32
-    )
-    scale_row = lax.rsqrt(deg_v[...].astype(F32))
-    hidden[col] = (hidden_t * scale_row).astype(BF16)
-
-    def hidden_copy(i, c, mate):
-        return remote(hidden.at[c], hidden.at[c], hid_ss.at[i], hid_rs.at[c], blk, mate)
-
-    def hidden_send(i, c, mate):
-        copy = hidden_copy(i, c, mate)
-        copy.start()
-        sends.append(copy)
-
-    hidden_send(0, col, over)
-    hidden_send(1, col, twin)
-
     def back_term(k, c):
-        return jnp.dot(
-            hidden[c], dense[k, pl.ds(c * rows, rows), :], preferred_element_type=F32
-        )
-
-    def back_first(k):
-        back[k] = back_term(k, col)
-
-    loop(span, back_first)
+        total = jnp.zeros((fin, rows), F32)
+        for h in range(2):
+            total += jnp.dot(
+                hidden[c, h],
+                dense[k, pl.ds(c * rows + h * side, side), :],
+                preferred_element_type=F32,
+            )
+        return total
 
     def back_more(c):
         def one(k):
@@ -338,27 +354,62 @@
 
         loop(span, one)
 
-    hidden_copy(0, twin, twin).wait_recv()
+    core = col % 2
+    piece = half // n_xy
+    for lo in range(2):
+        c = 2 * lo + core
+        remote(r1_send.at[c], r1_recv.at[c], r1_ss.at[0], r1_rs.at[lo], blk, twin).wait_recv()
+        total = r1_send[c] + r1_recv[c]
+        for i in range(n_xy):
+            r2_send[lo, i, :piece, :] = total[i * piece : (i + 1) * piece]
+            r2_send[lo, i, piece:, :] = total[half:]
+    r2_recv[col // 2, xy] = r2_send[col // 2, xy]
+    for i, (c, to, other) in enumerate(plane):
+        copy = remote(
+            r2_send.at[c // 2, to],
+            r2_recv.at[col // 2, xy],
+            r2_ss.at[i],
+            r2_rs.at[col // 2, xy],
+            other,
+            c,
+        )
+        copy.start()
+        sends.append(copy)
+
+    def back_first(k):
+        back[k] = back_term(k, col)
+
+    loop(span, back_first)
+
+    for h in range(2):
+        hidden_copy(0, over, h, over).wait_recv()
+        hidden_send(2, over, h, twin)
+    for h in range(2):
+        hidden_copy(0, twin, h, twin).wait_recv()
     back_more(twin)
-
-    for mate in mates:
-        remote(r1_send.at[mate], r1_recv.at[mate], r1_ss.at[0], r1_rs.at[mate], blk, mate).wait_recv()
-    total = r1_recv[0] + r1_recv[1] + r1_recv[2] + r1_recv[3]
-    piece = half // n_xy
-    for i in range(n_xy):
-        r2_send[i, :piece, :] = total[i * piece : (i + 1) * piece]
-        r2_send[i, piece:, :] = total[half:]
-    r2_recv[xy] = r2_send[xy]
-    for i, (to, other) in enumerate(xy_mates):
-        copy = remote(r2_send.at[to], r2_recv.at[xy], r2_ss.at[i], r2_rs.at[xy], other, col)
+    back_more(over)
+
+    for c, to, other in plane:
+        remote(
+            r2_send.at[c // 2, to],
+            r2_recv.at[c // 2, to],
+            r2_ss.at[0],
+            r2_rs.at[c // 2, to],
+            other,
+            c,
+        ).wait_recv()
+    total = jnp.zeros((piece + 8, fin), F32)
+    for lo in range(2):
+        for i in range(n_xy):
+            total = total + r2_recv[lo, i]
+    r3_recv[z] = total
+    for i, (to, other) in enumerate(z_mates):
+        copy = remote(r3_recv.at[z], r3_recv.at[z], r3_ss.at[i], r3_rs.at[z], other, col)
         copy.start()
         sends.append(copy)
 
-    hidden_copy(0, over, over).wait_recv()
-    hidden_send(2, over, twin)
-    back_more(over)
-
-    hidden_copy(0, across, across).wait_recv()
+    for h in range(2):
+        hidden_copy(0, across, h, across).wait_recv()
     back_copies = []
     for k in (1, 3, 0, 4):
         back_send[k] = (back[k] + back_term(k, across)).astype(BF16)
@@ -369,17 +420,6 @@
         back_copies.append(copy)
     sends += back_copies
 
-    for to, other in xy_mates:
-        remote(r2_send.at[to], r2_recv.at[to], r2_ss.at[0], r2_rs.at[to], other, col).wait_recv()
-    total = r2_recv[0]
-    for i in range(1, n_xy):
-        total = total + r2_recv[i]
-    r3_recv[z] = total
-    for i, (to, other) in enumerate(z_mates):
-        copy = remote(r3_recv.at[z], r3_recv.at[z], r3_ss.at[i], r3_rs.at[z], other, col)
-        copy.start()
-        sends.append(copy)
-
     back[reach] = back[reach] + back_term(reach, across)
 
     for to, other in z_mates:
@@ -387,9 +427,9 @@
     total = r3_recv[0]
     for i in range(1, n_z):
         total = total + r3_recv[i]
-    g1[xy] = total[:piece] * norm
-    for i, (to, other) in enumerate(xy_mates):
-        copy = remote(g1.at[xy], g1.at[xy], g1_ss.at[i], g1_rs.at[xy], other, col)
+    g2[col, xy] = total[:piece] * norm
+    for i, (c, to, other) in enumerate(plane):
+        copy = remote(g2.at[col, xy], g2.at[col, xy], g1_ss.at[i], g1_rs.at[col // 2, xy], other, c)
         copy.start()
         sends.append(copy)
     gb_out[:, :fin] = total[piece : piece + 1] * norm
@@ -402,20 +442,19 @@
             total = total + back_recv[k].astype(F32)
         gf_out[...] = jnp.transpose(total * lax.rsqrt(deg_v[...].astype(F32))).astype(BF16)
 
-    for to, other in xy_mates:
-        remote(g1.at[to], g1.at[to], g1_ss.at[0], g1_rs.at[to], other, col).wait_recv()
-    g2[col] = jnp.concatenate([g1[i] for i in range(n_xy)], axis=0)
-    for d, mate in enumerate(mates):
-        copy = remote(g2.at[col], g2.at[col], g2_ss.at[d], g2_rs.at[col], blk, mate)
+    for c, to, other in plane:
+        remote(g2.at[c, to], g2.at[c, to], g1_ss.at[0], g1_rs.at[c // 2, to], other, c).wait_recv()
+    for i, c in enumerate((col, over)):
+        copy = remote(g2.at[c], g2.at[c], g2_ss.at[i], g2_rs.at[c // 2], blk, twin)
         copy.start()
         sends.append(copy)
-
     finish_back()
-
-    for mate in mates:
-        remote(g2.at[mate], g2.at[mate], g2_ss.at[0], g2_rs.at[mate], blk, mate).wait_recv()
+    for c in (twin, across):
+        remote(g2.at[c], g2.at[c], g2_ss.at[0], g2_rs.at[c // 2], blk, twin).wait_recv()
     for c in range(COLS):
-        gw_out[(c % 2) * half : (c % 2 + 1) * half, (c // 2) * fin : (c // 2 + 1) * fin] = g2[c]
+        for i in range(n_xy):
+            top = (c % 2) * half + i * piece
+            gw_out[top : top + piece, (c // 2) * fin : (c // 2 + 1) * fin] = g2[c, i]
 
     for copy in sends:
         copy.wait_send()
@@ -495,41 +534,40 @@
             pltpu.SMEM((1, 2 * padded), jnp.int32),
             vmem((rows, fin), F32),
             vmem((span, rows, fin), BF16),
-            vmem((rows, fin), F32),
-            vmem((3, rows, fin), BF16),
-            vmem((3, rows, fin), BF16),
-            vmem((COLS, fin, rows), BF16),
+            vmem((2, rows // 2, fin), F32),
+            vmem((3, 2, rows // 2, fin), BF16),
+            vmem((3, 2, rows // 2, fin), BF16),
+            vmem((COLS, 2, fin, rows // 2), BF16),
             vmem((span, fin, rows), F32),
             vmem((span, fin, rows), BF16),
             vmem((span, fin, rows), BF16),
             vmem((COLS, half + 8, fin), F32),
             vmem((COLS, half + 8, fin), F32),
-            vmem((n_xy, piece + 8, fin), F32),
-            vmem((n_xy, piece + 8, fin), F32),
+            vmem((2, n_xy, piece + 8, fin), F32),
+            vmem((2, n_xy, piece + 8, fin), F32),
             vmem((n_z, piece + 8, fin), F32),
-            vmem((n_xy, piece, fin), F32),
-            vmem((COLS, half, fin), F32),
+            vmem((COLS, n_xy, piece, fin), F32),
             dma((8,)),
             dma((span,)),
             dma,
             dma((span,)),
             dma((span,)),
-            dma((3,)),
-            dma((3,)),
-            dma((3,)),
-            dma((COLS,)),
+            dma((3, 2)),
+            dma((3, 2)),
+            dma((3, 2)),
+            dma((COLS, 2)),
             dma((span,)),
             dma((span,)),
-            dma((3,)),
-            dma((COLS,)),
-            dma((n_xy - 1,)),
-            dma((n_xy,)),
+            dma((2,)),
+            dma((2,)),
+            dma((2 * n_xy - 1,)),
+            dma((2, n_xy)),
             dma((n_z - 1,)),
             dma((n_z,)),
-            dma((n_xy - 1,)),
-            dma((n_xy,)),
-            dma((3,)),
-            dma((COLS,)),
+            dma((2 * n_xy - 1,)),
+            dma((2, n_xy)),
+            dma((2,)),
+            dma((2,)),
         ],
         compiler_params=pltpu.CompilerParams(
             collective_id=0, has_side_effects=True, vmem_limit_bytes=52 * 2**20

time: 55.4 us -> 48.9 us (0.88)
  Pallas kernels: 54.7 us -> 48.2 us
    pallas_call x1, Pallas kernels: 53.9 us -> 47.4 us  [local(): pl.pallas_call(functools.partial(kernel, n_blk, n_z, norm), out_shape=out...]
where the time goes in v3:
time: 48.9 us; the launch traced here: 48.8 us
  Pallas kernels  48.2 us (99%)
  between operations  0.64 us (1%)
    pallas_call x1, Pallas kernels, local(): pl.pallas_call(functools.partial(kernel, n_blk, n_z, norm), out_shape=out...  47.4 us

profile of v3, /device:TPU:1, one launch (start us, length us, event | category | flops | bytes accessed | tf_op | source)
XLA Modules:
  0.0 48.8 jit_solution(4285966255938901298)
XLA Ops:
  0.6 47.4 %graph_layer.1 = (bf16[512,256]{1,0:T(8,128)(2,1)S(1)}, bf16[512,128]{1,0:T(8,128)(2,1)S(1)}, f32[128,256]{1,0:T(8,128)S(1)}, f32[1,256]{1,0:T(1,128)S(1)}) custom-call(s32[360]{0:T(512)} %tile_rows.1, s32[360]{0:T(512)} %tile_cols.1, s32[5]{0:T(128)} %counts.1, bf16[512,128]{1,0:T(8,128)(2,1)} %feats.1, s32[1,512]{1,0:T(1,128)} %bitcast.3, ...), custom_call_target="tpu_custom_call" | custom-call | tf_op jit(solution)/shard_map/graph_layer/pallas_call | solution.py:515
  48.0 0.8 %graph_results.1 = (bf16[512,256]{1,0:T(8,128)(2,1)}, bf16[512,128]{1,0:T(8,128)(2,1)}, f32[128,256]{1,0:T(8,128)}, f32[1,256]{1,0:T(1,128)}) custom-call(bf16[512,256]{1,0:T(8,128)(2,1)S(1)} %get-tuple-element.12.refs_0_, bf16[512,128]{1,0:T(8,128)(2,1)S(1)} %get-tuple-element.13.refs_1_, f32[128,256]{1,0:T(8,128)S(1)} %get-tuple-element.14.refs_2_, ...), custom_call_target="tpu_custom_call" | custom-call | tf_op jit(solution)/shard_map/graph_results/pallas_call | solution.py:577

commit v4 on v3

--- a/solution.py
+++ b/solution.py
@@ -13,6 +13,7 @@
 COLS = 4
 HI = 2
 ZLEN = 8
+WAYS = 3
 
 
 def remote(src, dst, send_sem, recv_sem, blk, col):
@@ -227,27 +228,36 @@
         )
     index_copy = pltpu.make_async_copy(index_v, index_s, index_sem)
     index_copy.start()
-    chain[slots] = jnp.zeros((tile, tile), F32)
+    for i in range(WAYS):
+        chain[i, slots] = jnp.zeros((tile, tile), F32)
     index_copy.wait()
 
-    def build(k):
-        tile_copy(k).wait()
+    def build(offsets):
+        for k in offsets:
+            tile_copy(k).wait()
 
         def slot(s):
-            chain[s] = tiles[k, s].astype(F32) + chain[index_s[0, k * slots + s]]
+            values = [
+                tiles[k, s].astype(F32) + chain[i, index_s[0, k * slots + s]]
+                for i, k in enumerate(offsets)
+            ]
+            for i, value in enumerate(values):
+                chain[i, s] = value
 
         loop(slots, slot)
 
         def row(r):
-            cells = [
-                chain[index_s[0, padded + (k * block_tiles + r) * dev_tiles + c]].astype(BF16)
-                for c in range(dev_tiles)
-            ]
-            dense[k, pl.ds(r * tile, tile), :] = jnp.concatenate(cells, axis=1)
+            for i, k in enumerate(offsets):
+                cells = [
+                    chain[i, index_s[0, padded + (k * block_tiles + r) * dev_tiles + c]].astype(BF16)
+                    for c in range(dev_tiles)
+                ]
+                dense[k, pl.ds(r * tile, tile), :] = jnp.concatenate(cells, axis=1)
 
         loop(block_tiles, row)
 
-    loop(span, build)
+    for first in range(0, span, WAYS):
+        build(range(first, min(first + WAYS, span)))
 
     for copy in arrivals:
         copy.wait_recv()
@@ -319,10 +329,13 @@
         scale_row = lax.rsqrt(deg_v[:, h * side : (h + 1) * side].astype(F32))
         hidden[col, h] = (hidden_t * scale_row).astype(BF16)
         hidden_send(0, col, h, over)
-        hidden_send(1, col, h, twin)
         act_out[h * side : (h + 1) * side] = (pre * gate).astype(BF16)
         part += jnp.dot(agg_t, low, preferred_element_type=F32)
         bias_part += jnp.sum(grad_pre, axis=0, keepdims=True)
+
+    copy = remote(hidden.at[col], hidden.at[col], hid_ss.at[1, 0], hid_rs.at[col, 0], blk, twin)
+    copy.start()
+    sends.append(copy)
 
     half = part.shape[0] // 2
     bias_rows = jnp.concatenate(
@@ -356,6 +369,7 @@
 
     core = col % 2
     piece = half // n_xy
+    used = pl.ds(0, piece + 2)
     for lo in range(2):
         c = 2 * lo + core
         remote(r1_send.at[c], r1_recv.at[c], r1_ss.at[0], r1_rs.at[lo], blk, twin).wait_recv()
@@ -366,8 +380,8 @@
     r2_recv[col // 2, xy] = r2_send[col // 2, xy]
     for i, (c, to, other) in enumerate(plane):
         copy = remote(
-            r2_send.at[c // 2, to],
-            r2_recv.at[col // 2, xy],
+            r2_send.at[c // 2, to, used],
+            r2_recv.at[col // 2, xy, used],
             r2_ss.at[i],
             r2_rs.at[col // 2, xy],
             other,
@@ -384,27 +398,26 @@
     for h in range(2):
         hidden_copy(0, over, h, over).wait_recv()
         hidden_send(2, over, h, twin)
-    for h in range(2):
-        hidden_copy(0, twin, h, twin).wait_recv()
+    remote(hidden.at[twin], hidden.at[twin], hid_ss.at[0, 0], hid_rs.at[twin, 0], blk, twin).wait_recv()
     back_more(twin)
     back_more(over)
 
     for c, to, other in plane:
         remote(
-            r2_send.at[c // 2, to],
-            r2_recv.at[c // 2, to],
+            r2_send.at[c // 2, to, used],
+            r2_recv.at[c // 2, to, used],
             r2_ss.at[0],
             r2_rs.at[c // 2, to],
             other,
             c,
         ).wait_recv()
-    total = jnp.zeros((piece + 8, fin), F32)
+    total = jnp.zeros((piece + 2, fin), F32)
     for lo in range(2):
         for i in range(n_xy):
-            total = total + r2_recv[lo, i]
-    r3_recv[z] = total
+            total = total + r2_recv[lo, i, used]
+    r3_recv[z, used] = total
     for i, (to, other) in enumerate(z_mates):
-        copy = remote(r3_recv.at[z], r3_recv.at[z], r3_ss.at[i], r3_rs.at[z], other, col)
+        copy = remote(r3_recv.at[z, used], r3_recv.at[z, used], r3_ss.at[i], r3_rs.at[z], other, col)
         copy.start()
         sends.append(copy)
 
@@ -423,10 +436,12 @@
     back[reach] = back[reach] + back_term(reach, across)
 
     for to, other in z_mates:
-        remote(r3_recv.at[to], r3_recv.at[to], r3_ss.at[0], r3_rs.at[to], other, col).wait_recv()
-    total = r3_recv[0]
+        remote(
+            r3_recv.at[to, used], r3_recv.at[to, used], r3_ss.at[0], r3_rs.at[to], other, col
+        ).wait_recv()
+    total = r3_recv[0, used]
     for i in range(1, n_z):
-        total = total + r3_recv[i]
+        total = total + r3_recv[i, used]
     g2[col, xy] = total[:piece] * norm
     for i, (c, to, other) in enumerate(plane):
         copy = remote(g2.at[col, xy], g2.at[col, xy], g1_ss.at[i], g1_rs.at[col // 2, xy], other, c)
@@ -519,7 +534,7 @@
         out_specs=(in_vmem,) * 4,
         scratch_shapes=[
             vmem((span, slots, tile, tile), BF16),
-            vmem((slots + 1, tile, tile), F32),
+            vmem((WAYS, slots + 1, tile, tile), F32),
             vmem((span, COLS * rows, rows), BF16),
             vmem((rows, fin), BF16),
             vmem((1, rows), jnp.int32),

time: 48.9 us -> 48.6 us (level)
  no operation moved by 1% of the time
where the time goes in v4:
time: 48.6 us; the launch traced here: 48.5 us
  Pallas kernels  47.9 us (99%)
  between operations  0.64 us (1%)
    pallas_call x1, Pallas kernels, local(): pl.pallas_call(functools.partial(kernel, n_blk, n_z, norm), out_shape=out...  47 us

profile of v4, /device:TPU:1, one launch (start us, length us, event | category | flops | bytes accessed | tf_op | source)
XLA Modules:
  0.0 48.5 jit_solution(2595959338941568573)
XLA Ops:
  0.6 47.0 %graph_layer.1 = (bf16[512,256]{1,0:T(8,128)(2,1)S(1)}, bf16[512,128]{1,0:T(8,128)(2,1)S(1)}, f32[128,256]{1,0:T(8,128)S(1)}, f32[1,256]{1,0:T(1,128)S(1)}) custom-call(s32[360]{0:T(512)} %tile_rows.1, s32[360]{0:T(512)} %tile_cols.1, s32[5]{0:T(128)} %counts.1, bf16[512,128]{1,0:T(8,128)(2,1)} %feats.1, s32[1,512]{1,0:T(1,128)} %bitcast.3, ...), custom_call_target="tpu_custom_call" | custom-call | tf_op jit(solution)/shard_map/graph_layer/pallas_call | solution.py:530
  47.7 0.8 %graph_results.1 = (bf16[512,256]{1,0:T(8,128)(2,1)}, bf16[512,128]{1,0:T(8,128)(2,1)}, f32[128,256]{1,0:T(8,128)}, f32[1,256]{1,0:T(1,128)}) custom-call(bf16[512,256]{1,0:T(8,128)(2,1)S(1)} %get-tuple-element.12.refs_0_, bf16[512,128]{1,0:T(8,128)(2,1)S(1)} %get-tuple-element.13.refs_1_, f32[128,256]{1,0:T(8,128)S(1)} %get-tuple-element.14.refs_2_, ...), custom_call_target="tpu_custom_call" | custom-call | tf_op jit(solution)/shard_map/graph_results/pallas_call | solution.py:592
